TPU v7x, 32 devices: a whole 2x2x4 slice. The times are simulated.
32 devices in a mesh: beam: 2 (over y), chan: 4 (over z), tile: 2 (over x), pol: 2 (over core).
Axes of the slice: x: 2, y: 2, z: 4, core: 2. Of those that a mesh axis runs over, the one named last changes fastest.
Arguments:
- voltages: bfloat16 [8, 32, 100000], P(('beam', 'tile', 'pol'), 'chan'), parts along dimension 0, may hold values from -6 to 6
- flagged: int32 [4, 32], P(('tile', 'pol'), 'chan'), may hold values 0 or 1
- channel_table: int32 [4], replicated, may hold values from 0 to 3, each once
Outputs:
- visibilities: float32 [2, 8, 128, 128], P(None, ('beam', 'chan'), ('tile', 'pol')), parts along dimension 1
There are 2 independent parts, one for each index of `beam`. A program takes and returns all parts, laid end to end along the dimension named above; an argument that names none is the same for every part. Nothing has to cross between parts.
Inputs may be any that keep to these rules, and one draw needn't show every extreme that they name: `flagged`: 1 marks an input whose spectra are zeroed. `channel_table`: a permutation of the 4 channel blocks.
All inputs are finite; a program needn't handle non-finite values. No bound on the sum of `flagged` on one device may be relied on, other than what follows from the above.
Results may differ from a plain program's by a relative error of at most 0.0012.
Values may be sent and summed in bfloat16 or wider, within the bound.
A program may use at most 64 MiB of HBM per device.

v0:
```python
import math
import jax
import jax.numpy as jnp
import numpy as np
from jax import lax
from jax.sharding import PartitionSpec as P

N_OUTER = 160
N_INNER = 125
TAPS = 4
FRAMES = 2


def window_table(tap_count, frame_len):
    position = np.arange(tap_count * frame_len) * 1.0
    centre = (position - tap_count * frame_len / 2.0 + 0.5) / frame_len
    shaped = np.sin(np.pi * centre) / (np.pi * centre)
    prototype = shaped * (
        0.5 - 0.5 * np.cos(2.0 * np.pi * (position + 0.5) / (tap_count * frame_len))
    )
    prototype = prototype / np.sqrt(np.sum(prototype * prototype) / frame_len)
    return prototype.reshape(tap_count, frame_len)


def make_spectra(samples_in, flags_in, channel_table, n_chan):
    in_dev = samples_in.shape[0]
    frame_len = N_OUTER * N_INNER
    half_len = N_OUTER // 2
    filt = jnp.asarray(window_table(TAPS, frame_len), jnp.float32)
    frames_all = samples_in.astype(jnp.float32).reshape(in_dev, FRAMES + TAPS - 1, frame_len)
    filtered = jnp.zeros((in_dev, FRAMES, frame_len), jnp.float32)
    for tap_index in range(TAPS):
        filtered = filtered + filt[tap_index] * frames_all[:, tap_index : tap_index + FRAMES]
    filtered = filtered.reshape(in_dev, FRAMES, N_INNER, N_OUTER)
    inner_idx = jnp.arange(N_INNER, dtype=jnp.int32)
    inner_ang = (
        2.0
        * math.pi
        / N_INNER
        * (inner_idx[:, None] * inner_idx[None, :] % N_INNER).astype(jnp.float32)
    )
    inner_mat = jnp.concatenate([jnp.cos(inner_ang), -jnp.sin(inner_ang)], axis=0)
    section_one = jnp.einsum("kn,vsnm->vskm", inner_mat, filtered, precision=lax.Precision.HIGH)
    real_one = section_one[:, :, :N_INNER]
    imag_one = section_one[:, :, N_INNER:]
    outer_idx = jnp.arange(N_OUTER, dtype=jnp.int32)
    twist_ang = (
        2.0
        * math.pi
        / frame_len
        * (inner_idx[:, None] * outer_idx[None, :] % frame_len).astype(jnp.float32)
    )
    twist_cos = jnp.cos(twist_ang)
    twist_sin = jnp.sin(twist_ang)
    real_two = real_one * twist_cos + imag_one * twist_sin
    imag_two = imag_one * twist_cos - real_one * twist_sin
    joined = jnp.concatenate([real_two, imag_two], axis=3)
    block_width = half_len // n_chan
    out_pos = jnp.arange(half_len, dtype=jnp.int32)
    owner = out_pos // block_width
    onehot = owner[:, None] == jnp.arange(n_chan, dtype=jnp.int32)[None, :]
    chosen = jnp.sum(jnp.where(onehot, channel_table[None, :], 0), axis=1)
    outer_k = chosen * block_width + out_pos % block_width
    outer_ang = (
        2.0
        * math.pi
        / N_OUTER
        * (outer_k[:, None] * outer_idx[None, :] % N_OUTER).astype(jnp.float32)
    )
    outer_cos = jnp.cos(outer_ang)
    outer_sin = jnp.sin(outer_ang)
    real_rows = jnp.concatenate([outer_cos, outer_sin], axis=1)
    imag_rows = jnp.concatenate([-outer_sin, outer_cos], axis=1)
    outer_mat = jnp.stack([real_rows, imag_rows], axis=0)
    spectrum = jnp.einsum("vskn,rjn->vrsjk", joined, outer_mat, precision=lax.Precision.HIGH)
    spectrum = spectrum.reshape(in_dev, 2, FRAMES, half_len * N_INNER)
    kept_mask = (1 - flags_in).astype(jnp.float32)
    spectrum = spectrum * (kept_mask[:, None, None, None] / math.sqrt(frame_len))
    return spectrum.astype(jnp.bfloat16)


def correlate(left_rows, panel_cols, scale):
    return (
        jnp.einsum("rik,jk->rij", left_rows, panel_cols, preferred_element_type=jnp.float32) * scale
    )


def on_device(voltages, flagged, channel_table):
    n_chan = lax.axis_size("chan")
    spectra = make_spectra(voltages[0], flagged[0], channel_table, n_chan)
    turned = lax.all_to_all(spectra, "chan", split_axis=3, concat_axis=0, tiled=True)
    group_len = turned.shape[0]
    chb_len = turned.shape[3]
    half_k = FRAMES * chb_len
    scale = 1.0 / math.sqrt(FRAMES * chb_len)
    band_rows = turned.reshape(group_len, 2 * half_k)
    swapped = jnp.concatenate([band_rows[:, half_k:], -band_rows[:, :half_k]], axis=1)
    left_rows = jnp.stack([band_rows, swapped], axis=0)
    vis_local = correlate(
        left_rows, lax.all_gather(band_rows, ("tile", "pol"), axis=0, tiled=True), scale
    )
    return vis_local[:, None]


def solution(mesh):
    in_specs = (P(("beam", "tile", "pol"), "chan", None), P(("tile", "pol"), "chan"), P())
    out_specs = P(None, ("beam", "chan"), ("tile", "pol"), None)
    return jax.shard_map(
        on_device, mesh=mesh, in_specs=in_specs, out_specs=out_specs, check_vma=False
    )
```

profile of v0, /device:TPU:0, one launch (start us, length us, event | category | flops | bytes accessed | tf_op | source)
XLA Modules:
  0.0 155.5 jit_solution(12879074996876843924)
XLA Ops:
  6.5 0.0 all-gather.2.cloned.1.call-start
  6.5 0.9 sine_negate_fusion
  7.5 1.0 fusion.38
  8.5 0.7 multiply_bitcast_fusion
  9.2 0.7 select_reduce_fusion
  9.9 1.1 fusion.42
  11.0 5.3 %reshape.90 = f32[8,5,20000]{2,1,0:T(8,128)} reshape(bf16[1,8,100000]{2,1,0:T(8,128)(2,1)} %param.4) | data formatting | bytes 4800000 | tf_op jit(solution)/shard_map/convert_element_type | solution.py:30
  16.3 10.0 %fusion.57 = (f32[8,2,20000]{2,1,0:T(2,128)S(1)}, f32[8,2,20000]{2,1,0:T(2,128)S(1)}, f32[8,2,20000]{2,1,0:T(2,128)S(1)}, f32[8,2,20000]{2,1,0:T(2,128)S(1)}) fusion(f32[8,5,20000]{2,1,0:T(8,128)} %reshape.90), kind=kLoop, calls=%fused_computation.76 | loop fusion | bytes 10240000 | tf_op jit(solution)/shard_map/slice | solution.py:33
  26.4 0.0 copy-done.3
  26.4 0.0 copy-done.4
  26.4 0.0 copy-done.5
  26.4 0.5 fusion.15
  26.9 1.3 reshape.87
  28.2 1.1 maximum_bitcast_fusion.9
  29.3 2.8 %fusion.7 = f32[8,2,250,160]{2,3,1,0:T(8,128)S(1)} fusion(f32[8,2,125,160]{3,2,0,1:T(8,128)S(1)} %reshape.87, f32[125,125]{1,0:T(8,128)} %get-tuple-element.18, f32[125,125]{1,0:T(8,128)} %get-tuple-element.19), kind=kOutput, calls=%fused_computation.8 | convolution fusion | flops 480031232 | bytes 3965000 | tf_op jit(solution)/shard_map/kn,vsnm->vskm/dot_general | solution.py:43
  32.1 0.7 multiply_add_fusion
  32.8 1.2 fusion.10
  34.1 1.7 %reshape.95 = f32[8,2,2,10000]{3,2,0,1:T(2,128)S(1)} reshape(f32[8,2,2,80,125]{4,3,2,0,1:T(8,128)S(1)} %fusion.10) | data formatting | bytes 2560000 | tf_op jit(solution)/shard_map/reshape | solution.py:76
  35.7 0.1 fusion.14
  35.9 16.1 %copy.32 = bf16[8,2,2,10000]{0,2,1,3:T(2,128)(2,1)} copy(bf16[8,2,2,10000]{3,0,2,1:T(8,128)(2,1)S(1)} %fusion.14) | data formatting | bytes 1280000 | tf_op jit(solution)/shard_map/convert_element_type | solution.py:79
  52.0 13.1 %reshape.96 = bf16[4,2,40000]{2,1,0:T(2,128)(2,1)S(1)} reshape(bf16[10000,2,2,8]{3,2,1,0:T(2,128)(2,1)} %bitcast.48) | data formatting | bytes 1280000
  65.2 23.1 %all_to_all.15 = bf16[4,2,40000]{2,1,0:T(2,128)(2,1)S(1)} all-to-all(bf16[4,2,40000]{2,1,0:T(2,128)(2,1)S(1)} %reshape.96), channel_id=1, replica_groups=mesh['beam'=2,'chan'=4,'tile'=2,'pol'=2] {'chan'}, dimensions={0} | all-to-all | bytes 1280000 | tf_op jit(solution)/shard_map/all_to_all | solution.py:91
  88.3 11.1 %reshape.97 = bf16[10000,2,2,8]{3,2,1,0:T(2,128)(2,1)} reshape(bf16[4,2,40000]{2,1,0:T(2,128)(2,1)S(1)} %all_to_all.15) | data formatting | bytes 1280000
  99.3 19.7 %copy.33 = bf16[8,2,2,4,2500]{4,2,1,0,3:T(2,128)(2,1)S(1)} copy(bf16[8,2,2,4,2500]{0,2,1,4,3:T(2,128)(2,1)} %bitcast.49) | data formatting | bytes 1280000 | tf_op jit(solution)/shard_map/all_to_all | solution.py:91
  119.1 1.5 reshape.89
  120.6 0.0 all-gather.2.cloned.1.call-update
  120.6 0.7 stack_reshape.3
  121.4 0.3 copy-done
  121.7 0.2 fusion.58
  121.9 0.2 maximum_bitcast_fusion.4
  122.0 23.3 %all-gather.2.cloned.1.call-done = bf16[128,10000]{1,0:T(8,128)(2,1)} async-done(((bf16[32,10000]{1,0:T(8,128)(2,1)}), bf16[128,10000]{1,0:T(8,128)(2,1)}) %all-gather.2.cloned.1.call-update) | async-done | bytes 2560016 | tf_op jit(solution)/shard_map/all_gather | solution.py:100
  145.3 3.4 %fusion.23 = f32[2,1,32,128]{3,2,1,0:T(8,128)} fusion(bf16[128,10000]{1,0:T(8,128)(2,1)} %all-gather.2.cloned.1.call-done, bf16[1,32,10000]{2,1,0:T(8,128)(2,1)S(1)} %maximum_bitcast_fusion.4, bf16[1,32,10000]{2,1,0:T(8,128)(2,1)S(1)} %stack_reshape.3), kind=kOutput, calls=%fused_computation.25 | convolution fusion | flops 164488192 | bytes 3872768 | tf_op jit(solution)/shard_map/rik,jk->rij/dot_general | solution.py:84
  (12 shorter events, 0.0 us)
Async XLA Ops:
  6.5 138.7 %all-gather.2.cloned.1.call-start = ((), (), s32[]{:S(2)}) async-start(), calls=%async_computation.1 | async-start | bytes 3235840 | tf_op jit(solution)/shard_map/all_gather | solution.py:100
  16.3 10.1 %copy-start.3 = (f32[20000]{0:T(1024)S(1)}, f32[20000]{0:T(1024)}, u32[]{:S(2)}) copy-start(f32[20000]{0:T(1024)} %constant.79) | copy-start | bytes 240004
  16.3 10.1 %copy-start.4 = (f32[20000]{0:T(1024)S(1)}, f32[20000]{0:T(1024)}, u32[]{:S(2)}) copy-start(f32[20000]{0:T(1024)} %constant.77) | copy-start | bytes 240004
  16.3 10.1 %copy-start.5 = (f32[20000]{0:T(1024)S(1)}, f32[20000]{0:T(1024)}, u32[]{:S(2)}) copy-start(f32[20000]{0:T(1024)} %constant.75) | copy-start | bytes 240004
  16.3 10.1 %copy-start.6 = (f32[20000]{0:T(1024)S(1)}, f32[20000]{0:T(1024)}, u32[]{:S(2)}) copy-start(f32[20000]{0:T(1024)} %constant.73) | copy-start | bytes 240004
  29.3 2.8 %copy-start.1 = (f32[125,160]{0,1:T(8,128)S(1)}, f32[125,160]{0,1:T(8,128)}, u32[]{:S(2)}) copy-start(f32[125,160]{0,1:T(8,128)} %get-tuple-element.20) | copy-start | bytes 240004
  29.3 2.8 %copy-start.2 = (f32[125,160]{0,1:T(8,128)S(1)}, f32[125,160]{0,1:T(8,128)}, u32[]{:S(2)}) copy-start(f32[125,160]{0,1:T(8,128)} %get-tuple-element.21) | copy-start | bytes 240004
  120.6 1.1 copy-start
Sparse Core Ops, SparseCore 0:
  120.8 24.4 all-gather.1
where the time goes:
time: 156 us; the launch traced here: 155 us
  local copies, waits for them, and re-layouts  81 us (52%)
  waiting for transfers between devices  23.3 us (15%)
  blocking collectives  23.1 us (15%)
  between operations  13.5 us (9%)
  matrix products  7.41 us (5%)
  other arithmetic  7.17 us (5%)
    unnamed x16, local copies, waits for them, and re-layouts  24.6 us
    all_gather x1, waiting for transfers between devices, on_device(): lax.all_gather(band_rows, ('tile', 'pol'), axis=0, tiled=True)  23.3 us
    all_to_all x1, blocking collectives, on_device(): lax.all_to_all(spectra, 'chan', split_axis=3, concat_axis=0, tiled=True)  23.1 us
    all_to_all x1, local copies, waits for them, and re-layouts, on_device(): lax.all_to_all(spectra, 'chan', split_axis=3, concat_axis=0, tiled=True)  19.7 us
    convert_element_type x1, local copies, waits for them, and re-layouts, make_spectra(): return spectrum.astype(jnp.bfloat16)  16.1 us
    slice x1, local copies, waits for them, and re-layouts, make_spectra(): frames_all[:, tap_index:tap_index + FRAMES]  10 us
    convert_element_type x1, local copies, waits for them, and re-layouts, make_spectra(): samples_in.astype(jnp.float32).reshape(in_dev, FRAMES + TAPS - 1, frame_len)  5.31 us
    dot_general x1, matrix products, correlate(): jnp.einsum('rik,jk->rij', left_rows, panel_cols, preferred_element_type=j...  3.36 us
  transfers between devices with their start and end apart: 1, of which 1 were waited for; matrix products, arithmetic and copies ran while one was open for 1% of the time, Pallas kernels for 0%

commit v1 on v0

--- a/solution.py
+++ b/solution.py
@@ -9,6 +9,23 @@
 N_INNER = 125
 TAPS = 4
 FRAMES = 2
+
+
+def joined_along(pieces, dim):
+    lengths = list(pieces.shape[1:])
+    lengths[dim] *= pieces.shape[0]
+    return jnp.moveaxis(pieces, 0, dim).reshape(lengths)
+
+
+def gather_around(shard, axis, dim):
+    devices = lax.axis_size(axis)
+    right = [(i, (i + 1) % devices) for i in range(devices)]
+    parts = [shard]
+    while len(parts) < devices:
+        parts.append(lax.ppermute(parts[-1], axis, right))
+    index = lax.axis_index(axis)
+    parts = jnp.stack(parts)[(index - jnp.arange(devices)) % devices]
+    return joined_along(parts, dim)
 
 
 def window_table(tap_count, frame_len):
@@ -96,9 +113,7 @@
     band_rows = turned.reshape(group_len, 2 * half_k)
     swapped = jnp.concatenate([band_rows[:, half_k:], -band_rows[:, :half_k]], axis=1)
     left_rows = jnp.stack([band_rows, swapped], axis=0)
-    vis_local = correlate(
-        left_rows, lax.all_gather(band_rows, ("tile", "pol"), axis=0, tiled=True), scale
-    )
+    vis_local = correlate(left_rows, gather_around(band_rows, ("tile", "pol"), 0), scale)
     return vis_local[:, None]
 
 

time: 156 us -> 148 us (0.949)
  between operations: 13.5 us -> 0.2 us
  waiting for transfers between devices: 23.3 us -> 28.2 us
    ppermute x0 -> x3, waiting for transfers between devices: none -> 28.2 us  [gather_around(): parts.append(lax.ppermute(parts[-1], axis, right))]
    all_gather x1 -> x0, waiting for transfers between devices: 23.3 us -> none  [on_device(): lax.all_gather(band_rows, ('tile', 'pol'), axis=0, tiled=True)]
    gather x0 -> x1, local copies, waits for them, and re-layouts: none -> 2.31 us  [gather_around(): parts = jnp.stack(parts)[(index - jnp.arange(devices)) % devices]]
    unnamed x16 -> x14, local copies, waits for them, and re-layouts: 24.6 us -> 24.2 us
  transfers between devices with their start and end apart: 1 -> 3, of which waited for: 1 -> 3; matrix products, arithmetic and copies ran while one was open for 1% -> 1% of each run, Pallas kernels for 0% -> 0%
where the time goes in v1:
time: 148 us; the launch traced here: 147 us
  local copies, waits for them, and re-layouts  81.9 us (55%)
  waiting for transfers between devices  28.2 us (19%)
  blocking collectives  23.1 us (16%)
  matrix products  7.59 us (5%)
  other arithmetic  5.9 us (4%)
    ppermute x3, waiting for transfers between devices, gather_around(): parts.append(lax.ppermute(parts[-1], axis, right))  28.2 us
    unnamed x14, local copies, waits for them, and re-layouts  24.2 us
    all_to_all x1, blocking collectives, on_device(): lax.all_to_all(spectra, 'chan', split_axis=3, concat_axis=0, tiled=True)  23.1 us
    all_to_all x1, local copies, waits for them, and re-layouts, on_device(): lax.all_to_all(spectra, 'chan', split_axis=3, concat_axis=0, tiled=True)  19.7 us
    convert_element_type x1, local copies, waits for them, and re-layouts, make_spectra(): return spectrum.astype(jnp.bfloat16)  16.2 us
    slice x1, local copies, waits for them, and re-layouts, make_spectra(): frames_all[:, tap_index:tap_index + FRAMES]  9.79 us
    convert_element_type x1, local copies, waits for them, and re-layouts, make_spectra(): samples_in.astype(jnp.float32).reshape(in_dev, FRAMES + TAPS - 1, frame_len)  5.31 us
    dot_general x1, matrix products, correlate(): jnp.einsum('rik,jk->rij', left_rows, panel_cols, preferred_element_type=j...  3.57 us
  transfers between devices with their start and end apart: 3, of which 3 were waited for; matrix products, arithmetic and copies ran while one was open for 1% of the time, Pallas kernels for 0%

profile of v1, /device:TPU:0, one launch (start us, length us, event | category | flops | bytes accessed | tf_op | source)
XLA Modules:
  0.0 146.9 jit_solution(12678527764755539859)
XLA Ops:
  0.0 0.9 sine_negate_fusion
  0.9 0.3 fusion.33
  1.3 5.3 %reshape.143 = f32[8,5,20000]{2,1,0:T(8,128)} reshape(bf16[1,8,100000]{2,1,0:T(8,128)(2,1)} %param.4) | data formatting | bytes 4800000 | tf_op jit(solution)/shard_map/convert_element_type | solution.py:47
  6.6 9.8 %fusion.54 = (f32[8,2,20000]{2,1,0:T(2,128)S(1)}, f32[8,2,20000]{2,1,0:T(2,128)S(1)}, f32[8,2,20000]{2,1,0:T(2,128)S(1)}, f32[8,2,20000]{2,1,0:T(2,128)S(1)}) fusion(f32[8,5,20000]{2,1,0:T(8,128)} %reshape.143), kind=kLoop, calls=%fused_computation.84 | loop fusion | bytes 10240000 | tf_op jit(solution)/shard_map/slice | solution.py:50
  16.5 0.5 fusion.14
  17.0 0.0 copy-start.4
  17.0 1.3 reshape.139
  18.3 0.1 select_reduce_fusion
  18.4 0.4 fusion.37
  18.8 2.8 %fusion.5 = f32[8,2,250,160]{2,3,1,0:T(8,128)S(1)} fusion(f32[8,2,125,160]{3,2,0,1:T(8,128)S(1)} %reshape.139, f32[125,125]{1,0:T(8,128)} %get-tuple-element.18, f32[125,125]{1,0:T(8,128)} %get-tuple-element.19), kind=kOutput, calls=%fused_computation.8 | convolution fusion | flops 480031232 | bytes 3965000 | tf_op jit(solution)/shard_map/kn,vsnm->vskm/dot_general | solution.py:60
  21.6 0.7 multiply_add_fusion
  22.3 0.1 maximum_bitcast_fusion.9
  22.4 1.3 fusion.8
  23.6 0.0 copy-start.5
  23.6 1.7 %reshape.156 = f32[8,2,2,10000]{3,2,0,1:T(2,128)S(1)} reshape(f32[8,2,2,80,125]{4,3,2,0,1:T(8,128)S(1)} %fusion.8) | data formatting | bytes 2560000 | tf_op jit(solution)/shard_map/reshape | solution.py:93
  25.3 0.1 fusion.13
  25.5 16.2 %copy.37 = bf16[8,2,2,10000]{0,2,1,3:T(2,128)(2,1)} copy(bf16[8,2,2,10000]{3,0,2,1:T(8,128)(2,1)S(1)} %fusion.13) | data formatting | bytes 1280000 | tf_op jit(solution)/shard_map/convert_element_type | solution.py:96
  41.6 13.1 %reshape.157 = bf16[4,2,40000]{2,1,0:T(2,128)(2,1)S(1)} reshape(bf16[10000,2,2,8]{3,2,1,0:T(2,128)(2,1)} %bitcast.50) | data formatting | bytes 1280000
  54.8 23.1 %all_to_all.15 = bf16[4,2,40000]{2,1,0:T(2,128)(2,1)S(1)} all-to-all(bf16[4,2,40000]{2,1,0:T(2,128)(2,1)S(1)} %reshape.157), channel_id=1, replica_groups=mesh['beam'=2,'chan'=4,'tile'=2,'pol'=2] {'chan'}, dimensions={0} | all-to-all | bytes 1280000 | tf_op jit(solution)/shard_map/all_to_all | solution.py:108
  77.9 11.1 %reshape.158 = bf16[10000,2,2,8]{3,2,1,0:T(2,128)(2,1)} reshape(bf16[4,2,40000]{2,1,0:T(2,128)(2,1)S(1)} %all_to_all.15) | data formatting | bytes 1280000
  89.0 19.7 %copy.38 = bf16[8,2,2,4,2500]{4,2,1,0,3:T(2,128)(2,1)S(1)} copy(bf16[8,2,2,4,2500]{0,2,1,4,3:T(2,128)(2,1)} %bitcast.51) | data formatting | bytes 1280000 | tf_op jit(solution)/shard_map/all_to_all | solution.py:108
  108.7 0.7 reshape.141
  109.4 0.1 collective-permute-start
  109.5 0.7 stack_reshape.4
  110.3 9.3 %collective-permute-done = bf16[32,10000]{1,0:T(8,128)(2,1)} collective-permute-done((bf16[32,10000]{1,0:T(8,128)(2,1)S(1)}, bf16[32,10000]{1,0:T(8,128)(2,1)}, u32[]{:S(2)}, u32[]{:S(2)}) %collective-permute-start) | collective-permute-done | bytes 640032 | tf_op jit(solution)/shard_map/ppermute | solution.py:25
  119.5 0.2 fusion.55
  119.7 10.0 %collective-permute-done.1 = bf16[32,10000]{1,0:T(8,128)(2,1)S(1)} collective-permute-done((bf16[32,10000]{1,0:T(8,128)(2,1)}, bf16[32,10000]{1,0:T(8,128)(2,1)S(1)}, u32[]{:S(2)}, u32[]{:S(2)}) %collective-permute-start.1) | collective-permute-done | bytes 640032 | tf_op jit(solution)/shard_map/ppermute | solution.py:25
  129.7 1.0 maximum_bitcast_fusion.4
  130.6 8.9 %collective-permute-done.2 = bf16[32,10000]{1,0:T(8,128)(2,1)S(1)} collective-permute-done((bf16[32,10000]{1,0:T(8,128)(2,1)S(1)}, bf16[32,10000]{1,0:T(8,128)(2,1)S(1)}, u32[]{:S(2)}, u32[]{:S(2)}) %collective-permute-start.2) | collective-permute-done | bytes 640032 | tf_op jit(solution)/shard_map/ppermute | solution.py:25
  139.6 1.5 %pad_maximum_fusion = bf16[4,32,10000]{2,1,0:T(8,128)(2,1)S(1)} fusion(bf16[1,32,10000]{2,1,0:T(8,128)(2,1)S(1)} %bitcast.56, bf16[1,32,10000]{2,1,0:T(8,128)(2,1)S(1)} %bitcast.55, bf16[1,32,10000]{2,1,0:T(8,128)(2,1)} %bitcast.13, bf16[1,32,10000]{2,1,0:T(8,128)(2,1)S(1)} %stack_reshape.4), kind=kLoop, calls=%fused_computation.5 | loop fusion | flops 3840000 | bytes 5120000 | tf_op jit(solution)/shard_map/stack | solution.py:27
  141.0 2.3 %gather_fusion = bf16[4,32,10000]{2,1,0:T(8,128)(2,1)} fusion(bf16[4,32,10000]{2,1,0:T(8,128)(2,1)S(1)} %pad_maximum_fusion, s32[1024]{0:T(1024)S(1)} %pad_clamp_fusion), kind=kCustom, calls=%fused_computation | custom fusion | bytes 5120016 | tf_op jit(solution)/shard_map/gather | solution.py:27
  143.4 3.6 %fusion.20 = f32[2,1,32,128]{3,2,1,0:T(8,128)} fusion(bf16[128,10000,1]{1,0,2:T(8,128)(2,1)} %bitcast.52, bf16[1,32,10000]{2,1,0:T(8,128)(2,1)} %maximum_bitcast_fusion.4, bf16[1,32,10000]{2,1,0:T(8,128)(2,1)S(1)} %stack_reshape.4), kind=kOutput, calls=%fused_computation.26 | convolution fusion | flops 164488192 | bytes 3872768 | tf_op jit(solution)/shard_map/rik,jk->rij/dot_general | solution.py:101
  (17 shorter events, 0.1 us)
Async XLA Ops:
  6.6 9.8 %copy-start = (f32[20000]{0:T(1024)S(1)}, f32[20000]{0:T(1024)}, u32[]{:S(2)}) copy-start(f32[20000]{0:T(1024)} %constant.101) | copy-start | bytes 240004
  6.6 9.8 %copy-start.1 = (f32[20000]{0:T(1024)S(1)}, f32[20000]{0:T(1024)}, u32[]{:S(2)}) copy-start(f32[20000]{0:T(1024)} %constant.103) | copy-start | bytes 240004
  6.6 9.8 %copy-start.2 = (f32[20000]{0:T(1024)S(1)}, f32[20000]{0:T(1024)}, u32[]{:S(2)}) copy-start(f32[20000]{0:T(1024)} %constant.97) | copy-start | bytes 240004
  6.6 9.8 %copy-start.3 = (f32[20000]{0:T(1024)S(1)}, f32[20000]{0:T(1024)}, u32[]{:S(2)}) copy-start(f32[20000]{0:T(1024)} %constant.99) | copy-start | bytes 240004
  17.0 1.3 copy-start.4
  23.6 1.7 %copy-start.5 = (s32[1,8]{1,0:T(1,128)S(1)}, s32[1,8]{1,0:T(1,128)}, u32[]{:S(2)}) copy-start(s32[1,8]{1,0:T(1,128)} %param.5) | copy-start | bytes 100
  109.4 10.1 %collective-permute-start = (bf16[32,10000]{1,0:T(8,128)(2,1)S(1)}, bf16[32,10000]{1,0:T(8,128)(2,1)}, u32[]{:S(2)}, u32[]{:S(2)}) collective-permute-start(bf16[32,10000]{1,0:T(8,128)(2,1)S(1)} %reshape.141), channel_id=1, source_target_pairs={{0,1},{1,2},{2,3},{3,0},{4,5},{5,6},{6,7},{7,4},{8,9},{9,10},{10,1... | collective-permute-start | bytes 1920008 | tf_op jit(solution)/shard_map/ppermute | solution.py:25
  119.5 10.1 %collective-permute-start.1 = (bf16[32,10000]{1,0:T(8,128)(2,1)}, bf16[32,10000]{1,0:T(8,128)(2,1)S(1)}, u32[]{:S(2)}, u32[]{:S(2)}) collective-permute-start(bf16[32,10000]{1,0:T(8,128)(2,1)} %collective-permute-done), channel_id=1, source_target_pairs={{0,1},{1,2},{2,3},{3,0},{4,5},{5,6},{6,7},{7,4},{8,9},{9,10},{10,1... | collective-permute-start | bytes 1920008 | tf_op jit(solution)/shard_map/ppermute | solution.py:25
  129.6 9.9 %collective-permute-start.2 = (bf16[32,10000]{1,0:T(8,128)(2,1)S(1)}, bf16[32,10000]{1,0:T(8,128)(2,1)S(1)}, u32[]{:S(2)}, u32[]{:S(2)}) collective-permute-start(bf16[32,10000]{1,0:T(8,128)(2,1)S(1)} %collective-permute-done.1), channel_id=1, source_target_pairs={{0,1},{1,2},{2,3},{3,0},{4,5},{5,6},{6,7},{7,4},{8,9},{9,10},{10,1... | collective-permute-start | bytes 1920008 | tf_op jit(solution)/shard_map/ppermute | solution.py:25
